TPU v7x, 256 devices: a whole 4x4x8 slice. The times are simulated.
256 devices in a mesh: frame: 128 (over z, x, y), track: 2 (over core).
Axes of the slice: x: 4, y: 4, z: 8, core: 2. Of those that a mesh axis runs over, the one named last changes fastest.
Arguments:
- feature_maps: bfloat16 [256, 4096, 256], P('frame'), may hold values from -16 to 16
- query_frame: int32 [1024], P('track'), may hold values from 0 to 255
- query_pixel: int32 [2, 1024], P(None, 'track'), may hold values from 0 to 63
- conv_kernel: float32 [3, 512], replicated, may hold values from -3 to 3
- norm_gain: float32 [512], replicated, may hold values from 0.5 to 1.5
- w_in: bfloat16 [2048, 512], P('track'), may hold values from -0.25 to 0.25
- w_out: bfloat16 [2048, 256], P('track'), may hold values from -0.125 to 0.125
Outputs:
- coarse_points: float32 [2, 256, 1024], P(None, 'frame', 'track')
- refined_points: float32 [2, 256, 1024], P(None, 'frame', 'track')
All inputs are finite; a program needn't handle non-finite values.
Results may differ from a plain program's by a relative error of at most 0.0035.
The roundings to bfloat16 on the way count: a program that leaves them out, or rounds other values in their place, can miss the bound.
Values may be sent and summed in bfloat16 or wider, within the bound.
A program may use at most 128 MiB of HBM per device.

v0:
```python
import jax
import jax.numpy as jnp
from jax import lax
from jax.sharding import Mesh
from jax.sharding import PartitionSpec as P

C = 256
SIDE = 64
KT = 3
FRAME = ("z", "x", "y")


def soft_argmax(queries, frame_map):
    scores = jnp.einsum(
        "tc,pc->tp", queries, frame_map, preferred_element_type=jnp.float32
    ) * C ** (-0.5)
    peak = jnp.max(scores, axis=1, keepdims=True)
    expo = jnp.exp(scores - peak)
    weights = expo / jnp.sum(expo, axis=1, keepdims=True)
    centers = (jnp.arange(SIDE, dtype=jnp.float32) + 0.5) * (2.0 / SIDE) - 1.0
    rows = jnp.repeat(centers, SIDE)
    columns = jnp.tile(centers, SIDE)
    vertical = jnp.sum(weights * rows, axis=1)
    horizontal = jnp.sum(weights * columns, axis=1)
    return (weights, vertical, horizontal)


def local(feature_maps, query_frame, query_pixel, conv_kernel, norm_gain, w_in, w_out):
    frames_here = feature_maps.shape[0]
    index = lax.axis_index(FRAME)
    count = lax.axis_size(FRAME)
    w_in = lax.all_gather(w_in, "track", axis=0, tiled=True)
    w_out = lax.all_gather(w_out, "track", axis=0, tiled=True)
    flat_maps = feature_maps.reshape(-1, C)
    offset_frame = query_frame - index * frames_here
    owned = (offset_frame >= 0) & (offset_frame < frames_here)
    flat_rows = (
        jnp.clip(offset_frame, 0, frames_here - 1) * (SIDE * SIDE)
        + query_pixel[0] * SIDE
        + query_pixel[1]
    )
    queries = jnp.where(owned[:, None], flat_maps[flat_rows], 0)
    for axis in ("z", "x", "y"):
        queries = lax.psum(queries, axis)
    sampled_list = []
    coarse = []
    for slot in range(frames_here):
        weights, vertical, horizontal = soft_argmax(queries, feature_maps[slot])
        sampled_list.append(
            jnp.dot(
                weights.astype(jnp.bfloat16), feature_maps[slot], preferred_element_type=jnp.float32
            ).astype(jnp.bfloat16)
        )
        coarse.append(jnp.stack([vertical, horizontal], 0))
    from_left = lax.ppermute(sampled_list[-1], FRAME, [(i, i + 1) for i in range(count - 1)])
    from_right = lax.ppermute(sampled_list[0], FRAME, [(i + 1, i) for i in range(count - 1)])
    window = [from_left] + sampled_list + [from_right]
    inside = [(index > 0).astype(jnp.float32)] + [1.0] * frames_here
    inside += [(index < count - 1).astype(jnp.float32)]
    refined = []
    for slot in range(frames_here):
        read_part = 0.0
        query_part = 0.0
        for tap in range(KT):
            read_part = read_part + conv_kernel[tap, :C] * window[slot + tap].astype(jnp.float32)
            query_part = query_part + conv_kernel[tap, C:] * inside[slot + tap]
        query_part = query_part * queries.astype(jnp.float32)
        blended = jnp.concatenate([read_part, query_part], axis=-1)
        normed = (
            blended
            * lax.rsqrt(jnp.mean(blended * blended, axis=1, keepdims=True) + 1e-06)
            * norm_gain
        ).astype(jnp.bfloat16)
        hidden = jnp.einsum("rm,hm->rh", normed, w_in, preferred_element_type=jnp.float32)
        hidden = jax.nn.gelu(hidden).astype(jnp.bfloat16)
        update = jnp.dot(hidden, w_out, preferred_element_type=jnp.float32)
        updated = (blended[:, :C] + update).astype(jnp.bfloat16)
        _, vertical, horizontal = soft_argmax(updated, feature_maps[slot])
        refined.append(jnp.stack([vertical, horizontal], 0))
    return (jnp.stack(coarse, 1), jnp.stack(refined, 1))


def solution(mesh):
    sizes = {"y": 4, "x": 4}
    z = mesh.shape["frame"] // 16
    split = Mesh(
        mesh.devices.reshape(z, sizes["x"], sizes["y"], mesh.shape["track"]),
        ("z", "x", "y", "track"),
    )
    in_specs = (
        P(FRAME, None, None),
        P("track"),
        P(None, "track"),
        P(),
        P(),
        P("track", None),
        P("track", None),
    )
    out_specs = (P(None, FRAME, "track"), P(None, FRAME, "track"))
    return jax.shard_map(local, mesh=split, in_specs=in_specs, out_specs=out_specs, check_vma=False)
```

profile of v0, /device:TPU:126, one launch (start us, length us, event | category | flops | bytes accessed | tf_op | source)
XLA Modules:
  0.0 278.4 jit_solution(8686620003232133565)
XLA Ops:
  8.0 0.8 slice_multiply_fusion
  8.8 0.7 compare_and_fusion
  9.5 0.7 compare_select_fusion
  10.2 4.3 %gather_fusion = bf16[512,256]{1,0:T(8,128)(2,1)S(1)} fusion(bf16[8192,256]{1,0:T(8,128)(2,1)} %bitcast.56, s32[1024]{0:T(1024)S(1)} %pad_clamp_fusion), kind=kCustom, calls=%fused_computation | custom fusion | bytes 526336 | tf_op jit(solution)/shard_map/gather | solution.py:42
  14.6 0.7 broadcast_select_fusion
  15.4 73.4 %all-reduce.4.cloned.1.call-done = bf16[512,256]{0,1:T(8,128)(2,1)} async-done(((bf16[512,256]{0,1:T(8,128)(2,1)}), bf16[512,256]{0,1:T(8,128)(2,1)}) %all-reduce.4.cloned.1.call-update) | async-done | bytes 262160 | tf_op jit(solution)/shard_map/psum | solution.py:44
  89.0 47.2 %all-reduce.6.cloned.1.call-done = bf16[512,256]{0,1:T(8,128)(2,1)} async-done(((bf16[512,256]{0,1:T(8,128)(2,1)}), bf16[512,256]{0,1:T(8,128)(2,1)}) %all-reduce.6.cloned.1.call-update) | async-done | bytes 262160 | tf_op jit(solution)/shard_map/psum | solution.py:44
  136.3 0.5 all-gather.3.cloned.1.call-update
  136.8 0.5 all-gather.5.cloned.1.call-update
  137.4 0.8 multiply_add_fusion
  138.2 47.6 %all-reduce.8.cloned.1.call-done = bf16[512,256]{0,1:T(8,128)(2,1)} async-done(((bf16[512,256]{0,1:T(8,128)(2,1)}), bf16[512,256]{0,1:T(8,128)(2,1)}) %all-reduce.8.cloned.1.call-update) | async-done | bytes 262160 | tf_op jit(solution)/shard_map/psum | solution.py:44
  185.8 3.2 %multiply_reduce_fusion.10 = (f32[512]{0:T(512)S(1)}, f32[512,4096]{1,0:T(8,128)S(1)}) fusion(bf16[512,256]{0,1:T(8,128)(2,1)} %all-reduce.8.cloned.1.call-done, bf16[2,4096,256]{2,1,0:T(8,128)(2,1)} %param.7), kind=kOutput, calls=%fused_computation.15 | convolution fusion | flops 1077935616 | bytes 10749952 | tf_op jit(solution)/shard_map/tc,pc->tp/dot_general | solution.py:14
  189.0 1.5 fusion.3
  190.6 2.2 fusion.54
  192.8 5.9 %collective-permute-start = (bf16[512,256]{0,1:T(8,128)(2,1)S(1)}, bf16[512,256]{0,1:T(8,128)(2,1)S(1)}, u32[]{:S(2)}, u32[]{:S(2)}) collective-permute-start(bf16[512,256]{0,1:T(8,128)(2,1)S(1)} %fusion.54), channel_id=1, source_target_pairs={{0,2},{2,4},{4,6},{6,8},{8,10},{10,12},{12,14},{14,16},{16,18},{18... | collective-permute-start | bytes 786440 | tf_op jit(solution)/shard_map/ppermute | solution.py:55
  198.7 1.4 multiply_reduce_fusion.11
  200.1 1.5 fusion.1
  201.6 2.2 fusion.59
  203.8 2.1 collective-permute-start.1
  206.4 11.1 %collective-permute-done.1 = bf16[512,256]{0,1:T(8,128)(2,1)S(1)} collective-permute-done((bf16[512,256]{0,1:T(8,128)(2,1)S(1)}, bf16[512,256]{0,1:T(8,128)(2,1)S(1)}, u32[]{:S(2)}, u32[]{:S(2)}) %collective-permute-start.1) | collective-permute-done | bytes 262176 | tf_op jit(solution)/shard_map/ppermute | solution.py:56
  217.5 0.3 fusion.77
  217.8 0.2 multiply_reduce_fusion.12
  218.1 5.0 %fusion.79 = f32[512,2048]{1,0:T(8,128)} fusion(bf16[2048,512]{1,0:T(8,128)(2,1)} %all-gather.3.cloned.1.call-done, f32[512,256]{0,1:T(8,128)S(1)} %get-tuple-element.20, f32[512,256]{0,1:T(8,128)S(1)} %get-tuple-element.18, f32[512]{0:T(512)S(1)} %add_rsqrt_fusion, f32[512]{0:T(512)S(1)} %copy-done.6), kind=kOutput, calls=%fused_computation.88 | convolution fusion | flops 1074790400 | bytes 7344128 | tf_op jit(solution)/shard_map/rm,hm->rh/dot_general | solution.py:74
  223.2 9.4 %multiply_reduce_fusion.8 = (f32[512]{0:T(512)S(1)}, f32[512,4096]{1,0:T(8,128)}) fusion(bf16[2,4096,256]{2,1,0:T(8,128)(2,1)} %param.7, f32[512,256]{0,1:T(8,128)S(1)} %get-tuple-element.18, bf16[2048,256]{1,0:T(8,128)(2,1)} %all-gather.5.cloned.1.call-done, f32[512,2048]{1,0:T(8,128)} %fusion.79), kind=kOutput, calls=%fused_computation.13 | convolution fusion | flops 1624505856 | bytes 16254976 | tf_op jit(solution)/shard_map/tc,pc->tp/dot_general | solution.py:14
  232.5 5.0 %fusion.7 = f32[512]{0:T(512)S(1)} fusion(f32[512,4096]{1,0:T(8,128)} %get-tuple-element.36, f32[512]{0:T(512)S(1)} %get-tuple-element.35), kind=kLoop, calls=%fused_computation.24 | loop fusion | flops 6290944 | bytes 8392704 | tf_op jit(solution)/shard_map/reduce_sum | solution.py:19
  237.6 3.5 %fusion.78 = f32[512,2048]{1,0:T(8,128)} fusion(bf16[2048,512]{1,0:T(8,128)(2,1)S(1)} %copy-done.4, f32[512,256]{0,1:T(8,128)S(1)} %get-tuple-element.21, f32[512,256]{0,1:T(8,128)S(1)} %get-tuple-element.19, f32[512]{0:T(512)S(1)} %copy-done.6, f32[512]{0:T(512)S(1)} %add_rsqrt_fusion.1), kind=kOutput, calls=%fused_computation.87 | convolution fusion | flops 1074790400 | bytes 7344128 | tf_op jit(solution)/shard_map/rm,hm->rh/dot_general | solution.py:74
  241.1 9.3 %multiply_reduce_fusion.9 = (f32[512]{0:T(512)S(1)}, f32[512,4096]{1,0:T(8,128)}) fusion(bf16[2,4096,256]{2,1,0:T(8,128)(2,1)} %param.7, f32[512,256]{0,1:T(8,128)S(1)} %get-tuple-element.19, bf16[2048,256]{1,0:T(8,128)(2,1)} %all-gather.5.cloned.1.call-done, f32[512,2048]{1,0:T(8,128)} %fusion.78), kind=kOutput, calls=%fused_computation.14 | convolution fusion | flops 1624505856 | bytes 16254976 | tf_op jit(solution)/shard_map/tc,pc->tp/dot_general | solution.py:14
  250.4 5.3 %fusion.5 = f32[512]{0:T(512)S(1)} fusion(f32[512,4096]{1,0:T(8,128)} %get-tuple-element.34, f32[512]{0:T(512)S(1)} %get-tuple-element.33), kind=kLoop, calls=%fused_computation.22 | loop fusion | flops 6290944 | bytes 8392704 | tf_op jit(solution)/shard_map/reduce_sum | solution.py:19
  255.7 0.5 copy-done.2
  256.2 13.8 %multiply_reduce_fusion.5 = (f32[512]{0:T(512)S(1)}, f32[512]{0:T(512)S(1)}, f32[512]{0:T(512)S(1)}, f32[512]{0:T(512)S(1)}, f32[512]{0:T(512)S(1)}, /*index=5*/f32[512]{0:T(512)S(1)}, f32[512]{0:T(512)S(1)}, f32[512]{0:T(512)S(1)}) fusion(f32[4096]{0:T(1024)S(1)} %mul.292, f32[4096]{0:T(1024)S(1)} %mul.295, f32[512]{0:T(512)S(1)} %fusion.5, ...), kind=kLoop, calls=%fused_computation.8 | loop fusion | flops 58716160 | bytes 33619968 | tf_op jit(solution)/shard_map/reduce_sum | solution.py:23
  270.1 0.6 copy.12
  270.7 0.6 copy.11
  (40 shorter events, 0.9 us)
Async XLA Ops:
  8.0 80.9 %all-reduce.4.cloned.1.call-start = ((), (), s32[]{:S(2)}) async-start(), calls=%async_computation | async-start | bytes 524288 | tf_op jit(solution)/shard_map/psum | solution.py:44
  15.4 120.8 %all-reduce.6.cloned.1.call-start = ((), (), s32[]{:S(2)}) async-start(), calls=%async_computation.1 | async-start | bytes 524288 | tf_op jit(solution)/shard_map/psum | solution.py:44
  88.9 96.9 %all-reduce.8.cloned.1.call-start = ((), (), s32[]{:S(2)}) async-start(), calls=%async_computation.2 | async-start | bytes 524288 | tf_op jit(solution)/shard_map/psum | solution.py:44
  136.2 81.9 %all-gather.3.cloned.1.call-start = ((), (), s32[]{:S(2)}) async-start(), calls=%async_computation.3 | async-start | bytes 3145728 | tf_op jit(solution)/shard_map/all_gather | solution.py:32
  136.8 86.4 %all-gather.5.cloned.1.call-start = ((), (), s32[]{:S(2)}) async-start(), calls=%async_computation.4 | async-start | bytes 1572864 | tf_op jit(solution)/shard_map/all_gather | solution.py:33
  185.8 4.7 %copy-start.3 = (bf16[2,4096,256]{2,1,0:T(8,128)(2,1)S(1)}, bf16[2,4096,256]{2,1,0:T(8,128)(2,1)}, u32[]{:S(2)}) copy-start(bf16[2,4096,256]{2,1,0:T(8,128)(2,1)} %param.7) | copy-start | bytes 12582916
  189.0 3.7 %copy-start = (f32[512,4096]{1,0:T(8,128)}, f32[512,4096]{1,0:T(8,128)S(1)}, u32[]{:S(2)}) copy-start(f32[512,4096]{1,0:T(8,128)S(1)} %get-tuple-element.30) | copy-start | bytes 25165828
  190.5 8.1 %copy-start.5 = (bf16[512,256]{0,1:T(8,128)(2,1)S(1)}, bf16[512,256]{0,1:T(8,128)(2,1)}, u32[]{:S(2)}) copy-start(bf16[512,256]{0,1:T(8,128)(2,1)} %all-reduce.8.cloned.1.call-done) | copy-start | bytes 786436
  192.8 13.6 %collective-permute-start = (bf16[512,256]{0,1:T(8,128)(2,1)S(1)}, bf16[512,256]{0,1:T(8,128)(2,1)S(1)}, u32[]{:S(2)}, u32[]{:S(2)}) collective-permute-start(bf16[512,256]{0,1:T(8,128)(2,1)S(1)} %fusion.54), channel_id=1, source_target_pairs={{0,2},{2,4},{4,6},{6,8},{8,10},{10,12},{12,14},{14,16},{16,18},{18... | collective-permute-start | bytes 786440 | tf_op jit(solution)/shard_map/ppermute | solution.py:55
  200.1 3.7 %copy-start.1 = (f32[512,4096]{1,0:T(8,128)}, f32[512,4096]{1,0:T(8,128)S(1)}, u32[]{:S(2)}) copy-start(f32[512,4096]{1,0:T(8,128)S(1)} %get-tuple-element.32) | copy-start | bytes 25165828
  201.6 16.5 %copy-start.6 = (f32[512]{0:T(512)S(1)}, f32[512]{0:T(512)}, u32[]{:S(2)}) copy-start(f32[512]{0:T(512)} %param.11) | copy-start | bytes 6148
  203.8 13.7 %collective-permute-start.1 = (bf16[512,256]{0,1:T(8,128)(2,1)S(1)}, bf16[512,256]{0,1:T(8,128)(2,1)S(1)}, u32[]{:S(2)}, u32[]{:S(2)}) collective-permute-start(bf16[512,256]{0,1:T(8,128)(2,1)S(1)} %fusion.59), channel_id=1, source_target_pairs={{2,0},{4,2},{6,4},{8,6},{10,8},{12,10},{14,12},{16,14},{18,16},{20... | collective-permute-start | bytes 786440 | tf_op jit(solution)/shard_map/ppermute | solution.py:56
  232.5 5.0 %copy-start.4 = (bf16[2048,512]{1,0:T(8,128)(2,1)S(1)}, bf16[2048,512]{1,0:T(8,128)(2,1)}, u32[]{:S(2)}) copy-start(bf16[2048,512]{1,0:T(8,128)(2,1)} %all-gather.3.cloned.1.call-done) | copy-start | bytes 6291460
  250.4 5.8 %copy-start.2 = (f32[512,4096]{1,0:T(8,128)S(1)}, f32[512,4096]{1,0:T(8,128)}, u32[]{:S(2)}) copy-start(f32[512,4096]{1,0:T(8,128)} %get-tuple-element.34) | copy-start | bytes 25165828
Sparse Core Ops, SparseCore 0:
  15.5 73.3 all-reduce.3
  91.3 44.8 all-reduce.5
  138.5 47.2 all-reduce.7
Sparse Core Ops, SparseCore 1:
  138.6 17.4 all-gather.2
  157.9 15.5 all-gather.4
where the time goes:
time: 279 us; the launch traced here: 278 us
  waiting for transfers between devices  181 us (65%)
  matrix products  36.3 us (13%)
  other arithmetic  31.5 us (11%)
  between operations  15.4 us (6%)
  starting transfers between devices  8.24 us (3%)
  local copies, waits for them, and re-layouts  6.37 us (2%)
    psum x3, waiting for transfers between devices, local(): queries = lax.psum(queries, axis)  168 us
    dot_general x4, matrix products, soft_argmax(): jnp.einsum('tc,pc->tp', queries, frame_map, preferred_element_type=jnp.fl...  23.3 us
    reduce_sum x1, other arithmetic, soft_argmax(): vertical = jnp.sum(weights * rows, axis=1)  13.8 us
    reduce_sum x4, other arithmetic, soft_argmax(): weights = expo / jnp.sum(expo, axis=1, keepdims=True)  13.3 us
    ppermute x1, waiting for transfers between devices, local(): lax.ppermute(sampled_list[0], FRAME, [(i + 1, i) for i in range(count - 1)])  11.1 us
    dot_general x2, matrix products, local(): jnp.einsum('rm,hm->rh', normed, w_in, preferred_element_type=jnp.float32)  8.57 us
    ppermute x1, starting transfers between devices, local(): lax.ppermute(sampled_list[-1], FRAME, [(i, i + 1) for i in range(count -...  5.9 us
  transfers between devices with their start and end apart: 7, of which 4 were waited for; matrix products, arithmetic and copies ran while one was open for 7% of the time, Pallas kernels for 0%

commit v1 on v0

--- a/solution.py
+++ b/solution.py
@@ -41,7 +41,12 @@
     )
     queries = jnp.where(owned[:, None], flat_maps[flat_rows], 0)
     for axis in ("z", "x", "y"):
-        queries = lax.psum(queries, axis)
+
+        def arrange_page_all(in_array, which_axis):
+            low = jax.lax.all_gather(in_array, which_axis)
+            return jnp.sum(low, axis=0)
+
+        queries = arrange_page_all(queries, axis)
     sampled_list = []
     coarse = []
     for slot in range(frames_here):

time: 279 us -> 208 us (0.75)
  waiting for transfers between devices: 181 us -> 106 us
  other arithmetic: 31.5 us -> 37.1 us
    psum x3 -> x0, waiting for transfers between devices: 168 us -> none  [local(): queries = lax.psum(queries, axis)]
    all_gather x0 -> x3, waiting for transfers between devices: none -> 92.8 us  [arrange_page_all(): low = jax.lax.all_gather(in_array, which_axis)]
    reduce_sum x0 -> x3, other arithmetic: none -> 6.29 us  [arrange_page_all(): return jnp.sum(low, axis=0)]
  transfers between devices with their start and end apart: 7 -> 7, of which waited for: 4 -> 4; matrix products, arithmetic and copies ran while one was open for 7% -> 9% of each run, Pallas kernels for 0% -> 0%
where the time goes in v1:
time: 208 us
  waiting for transfers between devices  106 us (51%)
  other arithmetic  37.1 us (18%)
  matrix products  36.3 us (17%)
  between operations  14 us (7%)
  starting transfers between devices  7.87 us (4%)
  local copies, waits for them, and re-layouts  6.75 us (3%)
    all_gather x3, waiting for transfers between devices, arrange_page_all(): low = jax.lax.all_gather(in_array, which_axis)  92.8 us
    dot_general x4, matrix products, soft_argmax(): jnp.einsum('tc,pc->tp', queries, frame_map, preferred_element_type=jnp.fl...  23.2 us
    reduce_sum x1, other arithmetic, soft_argmax(): vertical = jnp.sum(weights * rows, axis=1)  13.8 us
    reduce_sum x4, other arithmetic, soft_argmax(): weights = expo / jnp.sum(expo, axis=1, keepdims=True)  13.3 us
    ppermute x1, waiting for transfers between devices, local(): lax.ppermute(sampled_list[0], FRAME, [(i + 1, i) for i in range(count - 1)])  11.7 us
    dot_general x2, matrix products, local(): jnp.einsum('rm,hm->rh', normed, w_in, preferred_element_type=jnp.float32)  8.72 us
    reduce_sum x3, other arithmetic, arrange_page_all(): return jnp.sum(low, axis=0)  6.29 us
    ppermute x1, starting transfers between devices, local(): lax.ppermute(sampled_list[-1], FRAME, [(i, i + 1) for i in range(count -...  5.75 us
  transfers between devices with their start and end apart: 7, of which 4 were waited for; matrix products, arithmetic and copies ran while one was open for 9% of the time, Pallas kernels for 0%

profile of v1, /device:TPU:126, one launch (start us, length us, event | category | flops | bytes accessed | tf_op | source)
XLA Modules:
  0.0 207.7 jit_solution(1336732956706749837)
XLA Ops:
  7.2 0.8 slice_multiply_fusion
  8.0 0.7 compare_and_fusion
  8.7 0.7 compare_select_fusion
  9.4 4.3 %gather_fusion = bf16[512,256]{1,0:T(8,128)(2,1)S(1)} fusion(bf16[8192,256]{1,0:T(8,128)(2,1)} %bitcast.60, s32[1024]{0:T(1024)S(1)} %pad_clamp_fusion), kind=kCustom, calls=%fused_computation | custom fusion | bytes 526336 | tf_op jit(solution)/shard_map/gather | solution.py:42
  13.7 0.9 bitcast_select_fusion
  14.6 41.9 %all-gather.8.cloned.1.call-done = bf16[8,512,256]{2,1,0:T(8,128)(2,1)} async-done(((bf16[1,512,256]{2,1,0:T(8,128)(2,1)}), bf16[8,512,256]{2,1,0:T(8,128)(2,1)}) %all-gather.8.cloned.1.call-update) | async-done | bytes 2097168 | tf_op jit(solution)/shard_map/all_gather | solution.py:46
  56.6 2.7 %reduce_sum.162 = bf16[512,256]{1,0:T(8,128)(2,1)} reduce(bf16[8,512,256]{2,1,0:T(8,128)(2,1)} %all-gather.8.cloned.1.call-done, bf16[]{:T(256)} %constant.23.clone.1), dimensions={0}, to_apply=%region_0.1 | reduce | flops 917504 | bytes 2359298 | tf_op jit(solution)/shard_map/reduce_sum | solution.py:47
  59.3 25.1 %all-gather.14.cloned.1.call-done = bf16[2048,256]{1,0:T(8,128)(2,1)} async-done(((bf16[512,256]{1,0:T(8,128)(2,1)}), bf16[2048,256]{1,0:T(8,128)(2,1)}) %all-gather.14.cloned.1.call-update) | async-done | bytes 1048592 | tf_op jit(solution)/shard_map/all_gather | solution.py:46
  84.4 2.2 %reduce_sum.163 = bf16[512,256]{1,0:T(8,128)(2,1)} reduce(bf16[4,512,256]{2,1,0:T(8,128)(2,1)} %bitcast.62, bf16[]{:T(256)} %constant.23.clone.1), dimensions={0}, to_apply=%region_1.2 | reduce | flops 393216 | bytes 1310722 | tf_op jit(solution)/shard_map/reduce_sum | solution.py:47
  86.6 0.5 all-gather.10.cloned.1.call-update
  87.2 0.5 all-gather.12.cloned.1.call-update
  87.7 25.8 %all-gather.16.cloned.1.call-done = bf16[2048,256]{1,0:T(8,128)(2,1)} async-done(((bf16[512,256]{1,0:T(8,128)(2,1)}), bf16[2048,256]{1,0:T(8,128)(2,1)}) %all-gather.16.cloned.1.call-update) | async-done | bytes 1048592 | tf_op jit(solution)/shard_map/all_gather | solution.py:46
  113.5 1.5 reduce_sum.164
  115.0 3.1 %multiply_reduce_fusion.10 = (f32[512]{0:T(512)S(1)}, f32[512,4096]{1,0:T(8,128)S(1)}) fusion(bf16[512,256]{1,0:T(8,128)(2,1)S(1)} %reduce_sum.164, bf16[2,4096,256]{2,1,0:T(8,128)(2,1)} %param.7), kind=kOutput, calls=%fused_computation.15 | convolution fusion | flops 1077935616 | bytes 10749952 | tf_op jit(solution)/shard_map/tc,pc->tp/dot_general | solution.py:14
  118.1 1.4 multiply_reduce_fusion.11
  119.5 1.5 fusion.3
  121.4 2.2 %fusion.54 = bf16[512,256]{0,1:T(8,128)(2,1)S(1)} fusion(bf16[2,4096,256]{2,1,0:T(8,128)(2,1)S(1)} %copy-done.3, f32[512,4096]{1,0:T(8,128)S(1)} %get-tuple-element.34, f32[512]{0:T(512)S(1)} %fusion.3, f32[512]{0:T(512)S(1)} %get-tuple-element.33), kind=kOutput, calls=%fused_computation.67 | convolution fusion | flops 1082261504 | bytes 10752000 | tf_op jit(solution)/shard_map/dot_general | solution.py:55
  123.6 5.8 %collective-permute-start = (bf16[512,256]{0,1:T(8,128)(2,1)S(1)}, bf16[512,256]{0,1:T(8,128)(2,1)S(1)}, u32[]{:S(2)}, u32[]{:S(2)}) collective-permute-start(bf16[512,256]{0,1:T(8,128)(2,1)S(1)} %fusion.54), channel_id=1, source_target_pairs={{0,2},{2,4},{4,6},{6,8},{8,10},{10,12},{12,14},{14,16},{16,18},{18... | collective-permute-start | bytes 786440 | tf_op jit(solution)/shard_map/ppermute | solution.py:60
  129.3 1.5 fusion.1
  130.8 2.2 %fusion.59 = bf16[512,256]{0,1:T(8,128)(2,1)S(1)} fusion(bf16[2,4096,256]{2,1,0:T(8,128)(2,1)S(1)} %copy-done.3, f32[512,4096]{1,0:T(8,128)S(1)} %get-tuple-element.36, f32[512]{0:T(512)S(1)} %fusion.1, f32[512]{0:T(512)S(1)} %get-tuple-element.35), kind=kOutput, calls=%fused_computation.68 | convolution fusion | flops 1082261504 | bytes 10752000 | tf_op jit(solution)/shard_map/dot_general | solution.py:55
  133.1 1.9 collective-permute-start.1
  135.5 11.7 %collective-permute-done.1 = bf16[512,256]{0,1:T(8,128)(2,1)S(1)} collective-permute-done((bf16[512,256]{0,1:T(8,128)(2,1)S(1)}, bf16[512,256]{0,1:T(8,128)(2,1)S(1)}, u32[]{:S(2)}, u32[]{:S(2)}) %collective-permute-start.1) | collective-permute-done | bytes 262176 | tf_op jit(solution)/shard_map/ppermute | solution.py:61
  147.8 5.2 %fusion.79 = f32[512,2048]{1,0:T(8,128)} fusion(bf16[2048,512]{1,0:T(8,128)(2,1)} %all-gather.10.cloned.1.call-done, f32[512,256]{0,1:T(8,128)S(1)} %get-tuple-element.24, f32[512,256]{0,1:T(8,128)S(1)} %get-tuple-element.22, f32[512]{0:T(512)S(1)} %add_rsqrt_fusion, f32[512]{0:T(512)S(1)} %copy-done.5), kind=kOutput, calls=%fused_computation.88 | convolution fusion | flops 1074790400 | bytes 7344128 | tf_op jit(solution)/shard_map/rm,hm->rh/dot_general | solution.py:79
  153.0 9.4 %multiply_reduce_fusion.8 = (f32[512]{0:T(512)S(1)}, f32[512,4096]{1,0:T(8,128)}) fusion(bf16[2,4096,256]{2,1,0:T(8,128)(2,1)} %param.7, f32[512,256]{0,1:T(8,128)S(1)} %get-tuple-element.22, bf16[2048,256]{1,0:T(8,128)(2,1)} %all-gather.12.cloned.1.call-done, f32[512,2048]{1,0:T(8,128)} %fusion.79), kind=kOutput, calls=%fused_computation.13 | convolution fusion | flops 1624505856 | bytes 16254976 | tf_op jit(solution)/shard_map/tc,pc->tp/dot_general | solution.py:14
  162.4 5.0 %fusion.7 = f32[512]{0:T(512)S(1)} fusion(f32[512,4096]{1,0:T(8,128)} %get-tuple-element.40, f32[512]{0:T(512)S(1)} %get-tuple-element.39), kind=kLoop, calls=%fused_computation.24 | loop fusion | flops 6290944 | bytes 8392704 | tf_op jit(solution)/shard_map/reduce_sum | solution.py:19
  167.4 3.5 %fusion.78 = f32[512,2048]{1,0:T(8,128)} fusion(bf16[2048,512]{1,0:T(8,128)(2,1)S(1)} %copy-done.4, f32[512,256]{0,1:T(8,128)S(1)} %get-tuple-element.25, f32[512,256]{0,1:T(8,128)S(1)} %get-tuple-element.23, f32[512]{0:T(512)S(1)} %copy-done.5, f32[512]{0:T(512)S(1)} %add_rsqrt_fusion.1), kind=kOutput, calls=%fused_computation.87 | convolution fusion | flops 1074790400 | bytes 7344128 | tf_op jit(solution)/shard_map/rm,hm->rh/dot_general | solution.py:79
  171.0 9.3 %multiply_reduce_fusion.9 = (f32[512]{0:T(512)S(1)}, f32[512,4096]{1,0:T(8,128)}) fusion(bf16[2,4096,256]{2,1,0:T(8,128)(2,1)} %param.7, f32[512,256]{0,1:T(8,128)S(1)} %get-tuple-element.23, bf16[2048,256]{1,0:T(8,128)(2,1)} %all-gather.12.cloned.1.call-done, f32[512,2048]{1,0:T(8,128)} %fusion.78), kind=kOutput, calls=%fused_computation.14 | convolution fusion | flops 1624505856 | bytes 16254976 | tf_op jit(solution)/shard_map/tc,pc->tp/dot_general | solution.py:14
  180.3 5.2 %fusion.5 = f32[512]{0:T(512)S(1)} fusion(f32[512,4096]{1,0:T(8,128)} %get-tuple-element.38, f32[512]{0:T(512)S(1)} %get-tuple-element.37), kind=kLoop, calls=%fused_computation.22 | loop fusion | flops 6290944 | bytes 8392704 | tf_op jit(solution)/shard_map/reduce_sum | solution.py:19
  185.5 0.5 copy-done.2
  186.1 13.8 %multiply_reduce_fusion.5 = (f32[512]{0:T(512)S(1)}, f32[512]{0:T(512)S(1)}, f32[512]{0:T(512)S(1)}, f32[512]{0:T(512)S(1)}, f32[512]{0:T(512)S(1)}, /*index=5*/f32[512]{0:T(512)S(1)}, f32[512]{0:T(512)S(1)}, f32[512]{0:T(512)S(1)}) fusion(f32[4096]{0:T(1024)S(1)} %mul.292, f32[4096]{0:T(1024)S(1)} %mul.295, f32[512]{0:T(512)S(1)} %fusion.5, ...), kind=kLoop, calls=%fused_computation.8 | loop fusion | flops 58716160 | bytes 33619968 | tf_op jit(solution)/shard_map/reduce_sum | solution.py:23
  199.9 0.6 copy.19
  200.6 0.6 copy.18
  (43 shorter events, 1.8 us)
Async XLA Ops:
  7.2 80.6 %copy-start.6 = (f32[3,512]{1,0:T(4,128)S(1)}, f32[3,512]{1,0:T(4,128)}, u32[]{:S(2)}) copy-start(f32[3,512]{1,0:T(4,128)} %param.10) | copy-start | bytes 18436
  7.2 49.4 %all-gather.8.cloned.1.call-start = ((), (), s32[]{:S(2)}) async-start(), calls=%async_computation | async-start | bytes 2359296 | tf_op jit(solution)/shard_map/all_gather | solution.py:46
  14.6 69.8 %all-gather.14.cloned.1.call-start = ((), (), s32[]{:S(2)}) async-start(), calls=%async_computation.3 | async-start | bytes 1310720 | tf_op jit(solution)/shard_map/all_gather | solution.py:46
  59.2 54.3 %all-gather.16.cloned.1.call-start = ((), (), s32[]{:S(2)}) async-start(), calls=%async_computation.4 | async-start | bytes 1310720 | tf_op jit(solution)/shard_map/all_gather | solution.py:46
  86.5 61.3 %all-gather.10.cloned.1.call-start = ((), (), s32[]{:S(2)}) async-start(), calls=%async_computation.1 | async-start | bytes 3145728 | tf_op jit(solution)/shard_map/all_gather | solution.py:32
  87.1 65.9 %all-gather.12.cloned.1.call-start = ((), (), s32[]{:S(2)}) async-start(), calls=%async_computation.2 | async-start | bytes 1572864 | tf_op jit(solution)/shard_map/all_gather | solution.py:33
  115.0 3.1 %copy-start.3 = (bf16[2,4096,256]{2,1,0:T(8,128)(2,1)S(1)}, bf16[2,4096,256]{2,1,0:T(8,128)(2,1)}, u32[]{:S(2)}) copy-start(bf16[2,4096,256]{2,1,0:T(8,128)(2,1)} %param.7) | copy-start | bytes 12582916
  118.1 3.2 %copy-start = (f32[512,4096]{1,0:T(8,128)}, f32[512,4096]{1,0:T(8,128)S(1)}, u32[]{:S(2)}) copy-start(f32[512,4096]{1,0:T(8,128)S(1)} %get-tuple-element.34) | copy-start | bytes 25165828
  119.5 11.3 %copy-start.1 = (f32[512,4096]{1,0:T(8,128)}, f32[512,4096]{1,0:T(8,128)S(1)}, u32[]{:S(2)}) copy-start(f32[512,4096]{1,0:T(8,128)S(1)} %get-tuple-element.36) | copy-start | bytes 25165828
  123.6 12.0 %collective-permute-start = (bf16[512,256]{0,1:T(8,128)(2,1)S(1)}, bf16[512,256]{0,1:T(8,128)(2,1)S(1)}, u32[]{:S(2)}, u32[]{:S(2)}) collective-permute-start(bf16[512,256]{0,1:T(8,128)(2,1)S(1)} %fusion.54), channel_id=1, source_target_pairs={{0,2},{2,4},{4,6},{6,8},{8,10},{10,12},{12,14},{14,16},{16,18},{18... | collective-permute-start | bytes 786440 | tf_op jit(solution)/shard_map/ppermute | solution.py:60
  130.8 17.0 %copy-start.5 = (f32[512]{0:T(512)S(1)}, f32[512]{0:T(512)}, u32[]{:S(2)}) copy-start(f32[512]{0:T(512)} %param.11) | copy-start | bytes 6148
  133.1 14.2 %collective-permute-start.1 = (bf16[512,256]{0,1:T(8,128)(2,1)S(1)}, bf16[512,256]{0,1:T(8,128)(2,1)S(1)}, u32[]{:S(2)}, u32[]{:S(2)}) collective-permute-start(bf16[512,256]{0,1:T(8,128)(2,1)S(1)} %fusion.59), channel_id=1, source_target_pairs={{2,0},{4,2},{6,4},{8,6},{10,8},{12,10},{14,12},{16,14},{18,16},{20... | collective-permute-start | bytes 786440 | tf_op jit(solution)/shard_map/ppermute | solution.py:61
  162.4 5.0 %copy-start.4 = (bf16[2048,512]{1,0:T(8,128)(2,1)S(1)}, bf16[2048,512]{1,0:T(8,128)(2,1)}, u32[]{:S(2)}) copy-start(bf16[2048,512]{1,0:T(8,128)(2,1)} %all-gather.10.cloned.1.call-done) | copy-start | bytes 6291460
  180.3 5.8 %copy-start.2 = (f32[512,4096]{1,0:T(8,128)S(1)}, f32[512,4096]{1,0:T(8,128)}, u32[]{:S(2)}) copy-start(f32[512,4096]{1,0:T(8,128)} %get-tuple-element.38) | copy-start | bytes 25165828
Sparse Core Ops, SparseCore 0:
  14.7 41.8 all-gather.7
  59.4 24.9 all-gather.13
  86.7 26.8 all-gather.15
  115.2 17.2 all-gather.9
  134.1 15.6 all-gather.11
